TPU v7x, 32 devices: a whole 2x2x4 slice. The times are simulated.
32 devices in a mesh: gx: 8 (over z, x), gy: 4 (over y, core).
Axes of the slice: x: 2, y: 2, z: 4, core: 2. Of those that a mesh axis runs over, the one named last changes fastest.
Arguments:
- resident_rows: int32 [4, 8, 32768], P('gy', 'gx'), may hold values from 0 to 1023
- resident_columns: int32 [4, 8, 32768], P('gy', 'gx'), may hold values from 0 to 511
- resident_strength: float32 [3, 4, 8, 32768], P(None, 'gy', 'gx'), may hold values from -6 to 6
- crossing_rows: int32 [4, 8, 2048], P('gy', 'gx'), may hold values from 0 to 1023
- crossing_columns: int32 [4, 8, 2048], P('gy', 'gx'), may hold values from 0 to 511
- crossing_strength: float32 [3, 4, 8, 2048], P(None, 'gy', 'gx'), may hold values from -6 to 6
- crossing_count: int32 [4, 8], P('gy', 'gx'), may hold values from 512 to 2048, as said below
Outputs:
- vorticity_spectrum: float32 [2, 3, 1, 4096, 4096], P(None, None, None, 'gy', 'gx')
Inputs may be any that keep to these rules, and one draw needn't show every extreme that they name: `crossing_count`: in every draw at least one device has exactly 2048 live send slots.
All inputs are finite; a program needn't handle non-finite values.
Results may differ from a plain program's by a relative error of at most 0.0003.
Values sent between devices are 32-bit elements; how exact they have to be, the bound alone decides.
No kernel may reach another device: no remote copies, remote signals or barrier semaphores. Data moves between devices by JAX's collectives and lax.ppermute only.
A program may use at most 192 MiB of HBM per device.

v0:
```python
import math

import jax
import jax.numpy as jnp
from jax import lax
from jax.sharding import PartitionSpec as P

NX = 4096
NY = 4096
LEV = 1


TWO_PI = 2.0 * math.pi


def from_behind(value, axis, steps):
    count = lax.axis_size(axis)
    pairs = [(source, (source + steps) % count) for source in range(count)]
    return lax.ppermute(value, axis, pairs)


def partner_2(block, axis, stride):
    count = lax.axis_size(axis)
    route = []
    for low in range(count):
        high = low | 1 << stride
        if high != low and high < count:
            route += [(low, high), (high, low)]
    return lax.ppermute(block, axis, route)


def bit_reverse(slab_index, bit_count):
    result = jnp.zeros_like(slab_index)
    for level in range(bit_count):
        result = result | (slab_index >> level & 1) << bit_count - 1 - level
    return result


def section_mix(parts, partner, slab_index, bit_number):
    half_span = 1 << bit_number
    upper_half = slab_index >> bit_number & 1 == 1
    phase_angle = (slab_index & half_span - 1).astype(jnp.float32) * (-math.pi / half_span)
    cosine = jnp.cos(phase_angle)
    sine_value = jnp.sin(phase_angle)
    summed = parts + partner
    difference = partner - parts
    if parts.shape[0] == 1:
        summed = jnp.concatenate([summed, jnp.zeros_like(summed)])
        turned = jnp.concatenate([difference * cosine, difference * sine_value])
    else:
        turned = jnp.stack(
            [
                difference[0] * cosine - difference[1] * sine_value,
                difference[0] * sine_value + difference[1] * cosine,
            ]
        )
    return jnp.where(upper_half, turned, summed)


def local_table(k_first, slab_count, length):
    total = slab_count * length
    row_index = lax.broadcasted_iota(jnp.int32, (length, length), 0)
    col_index = lax.broadcasted_iota(jnp.int32, (length, length), 1)
    phase = col_index * (k_first + slab_count * row_index) % total
    phase_angle = phase.astype(jnp.float32) * (TWO_PI / total)
    return (jnp.cos(phase_angle), -jnp.sin(phase_angle))


def along_columns(parts, table_real, table_imag):

    def product(data, table):
        return jnp.einsum(
            "clyx,kx->clyk",
            data,
            table,
            precision=lax.Precision.HIGHEST,
            preferred_element_type=jnp.float32,
        )

    return jnp.stack(
        [
            product(parts[0], table_real) - product(parts[1], table_imag),
            product(parts[0], table_imag) + product(parts[1], table_real),
        ]
    )


def along_rows(parts, table_real, table_imag):

    def product(data, table):
        return jnp.einsum(
            "clyx,ky->clkx",
            data,
            table,
            precision=lax.Precision.HIGHEST,
            preferred_element_type=jnp.float32,
        )

    return jnp.stack(
        [
            product(parts[0], table_real) - product(parts[1], table_imag),
            product(parts[0], table_imag) + product(parts[1], table_real),
        ]
    )


def shards(
    resident_rows,
    resident_columns,
    resident_strength,
    crossing_rows,
    crossing_columns,
    crossing_strength,
    crossing_count,
):
    cells_x = NX // lax.axis_size("gx")
    cells_y = NY // lax.axis_size("gy")
    slot_count = crossing_rows.shape[-1]
    slot_index = lax.broadcasted_iota(jnp.int32, (1, slot_count), 1)
    live_slot = (slot_index < crossing_count).astype(jnp.float32)
    outgoing = jnp.concatenate(
        [
            crossing_rows.reshape(1, slot_count).astype(jnp.float32),
            crossing_columns.reshape(1, slot_count).astype(jnp.float32),
            crossing_strength.reshape(3, slot_count) * live_slot,
        ],
        axis=0,
    )
    arrived = from_behind(outgoing, "gx", 1)
    resident_ids = resident_rows.reshape(-1) * cells_x + resident_columns.reshape(-1)
    arrived_ids = arrived[0].astype(jnp.int32) * cells_x + arrived[1].astype(jnp.int32)
    cell_ids = jnp.concatenate([resident_ids, arrived_ids])
    weights = jnp.concatenate([resident_strength.reshape(3, -1), arrived[2:]], axis=1)
    cell_total = LEV * cells_y * cells_x
    deposited = jnp.stack(
        [
            jax.ops.segment_sum(weights[component], cell_ids, num_segments=cell_total)
            for component in range(3)
        ]
    )
    vorticity = deposited.reshape(1, 3, LEV, cells_y, cells_x) * (1.0 / math.sqrt(NX * NY))
    bits_x = lax.axis_size("gx").bit_length() - 1
    parts = vorticity
    slab_index = lax.axis_index("gx")
    for bit_number in range(bits_x - 1, -1, -1):
        partner = partner_2(parts, "gx", bit_number)
        parts = section_mix(parts, partner, slab_index, bit_number)
    table_real, table_imag = local_table(
        bit_reverse(lax.axis_index("gx"), bits_x), lax.axis_size("gx"), cells_x
    )
    parts = along_columns(parts, table_real, table_imag)
    bits_y = lax.axis_size("gy").bit_length() - 1
    slab_index = lax.axis_index("gy")
    for bit_number in range(bits_y - 1, -1, -1):
        partner = partner_2(parts, "gy", bit_number)
        parts = section_mix(parts, partner, slab_index, bit_number)
    table_real, table_imag = local_table(
        bit_reverse(lax.axis_index("gy"), bits_y), lax.axis_size("gy"), cells_y
    )
    return along_rows(parts, table_real, table_imag)


def solution(mesh):
    return jax.shard_map(
        shards,
        mesh=mesh,
        in_specs=(
            P("gy", "gx", None),
            P("gy", "gx", None),
            P(None, "gy", "gx", None),
            P("gy", "gx", None),
            P("gy", "gx", None),
            P(None, "gy", "gx", None),
            P("gy", "gx"),
        ),
        out_specs=P(None, None, None, "gy", "gx"),
        check_vma=False,
    )
```

profile of v0, /device:TPU:1, one launch (start us, length us, event | category | flops | bytes accessed | tf_op | source)
XLA Modules:
  0.0 2129.3 jit_solution(16955251792768350621)
XLA Ops:
  9.4 183.1 %scatter_custom_fusion = f32[524288]{0:T(1024)} fusion(s32[34816]{0:T(1024)S(1)} %pad_add_fusion, f32[34816]{0:T(1024)S(1)} %bitcast.88, f32[]{:T(128)} %constant.52.clone.1), kind=kCustom, calls=%fused_computation.69 | custom fusion | flops 34816 | bytes 2097156 | tf_op jit(solution)/shard_map/scatter-add | solution.py:137
  194.2 183.1 %scatter_custom_fusion.1 = f32[524288]{0:T(1024)} fusion(s32[34816]{0:T(1024)S(1)} %pad_add_fusion, f32[34816]{0:T(1024)S(1)} %bitcast.87, f32[]{:T(128)} %constant.52.clone.1), kind=kCustom, calls=%fused_computation.67 | custom fusion | flops 34816 | bytes 2097156 | tf_op jit(solution)/shard_map/scatter-add | solution.py:137
  380.1 183.3 %scatter_custom_fusion.2 = f32[524288]{0:T(1024)} fusion(s32[34816]{0:T(1024)S(1)} %pad_add_fusion, f32[34816]{0:T(1024)S(1)} %bitcast.86, f32[]{:T(128)} %constant.52.clone.1), kind=kCustom, calls=%fused_computation.65 | custom fusion | flops 34816 | bytes 2097156 | tf_op jit(solution)/shard_map/scatter-add | solution.py:137
  572.8 272.0 %collective-permute-done.1 = f32[1,3,1,1024,512]{4,3,1,2,0:T(8,128)} collective-permute-done((f32[1,3,1,1024,512]{4,3,1,2,0:T(8,128)}, f32[1,3,1,1024,512]{4,3,1,2,0:T(8,128)}, u32[]{:S(2)}, u32[]{:S(2)}) %collective-permute-start.1) | collective-permute-done | bytes 6291488 | tf_op jit(solution)/shard_map/ppermute | solution.py:29
  860.9 271.6 %collective-permute-done.2 = f32[2,3,1,1024,512]{4,3,1,2,0:T(8,128)} collective-permute-done((f32[2,3,1,1024,512]{4,3,1,2,0:T(8,128)}, f32[2,3,1,1024,512]{4,3,1,2,0:T(8,128)}, u32[]{:S(2)}, u32[]{:S(2)}) %collective-permute-start.2) | collective-permute-done | bytes 12582944 | tf_op jit(solution)/shard_map/ppermute | solution.py:29
  1132.4 16.6 fusion.86
  1163.4 15.7 maximum_select_fusion.1
  1179.1 270.8 %collective-permute-done.3 = f32[2,3,1,1024,512]{4,3,1,2,0:T(8,128)} collective-permute-done((f32[2,3,1,1024,512]{4,3,1,2,0:T(8,128)}, f32[2,3,1,1024,512]{4,3,1,2,0:T(8,128)}, u32[]{:S(2)}, u32[]{:S(2)}) %collective-permute-start.3) | collective-permute-done | bytes 12582944 | tf_op jit(solution)/shard_map/ppermute | solution.py:29
  1449.9 24.9 %fusion.87 = f32[2,3,1,1024,512]{4,3,1,2,0:T(8,128)} fusion(f32[2,3,1,1024,512]{4,3,1,2,0:T(8,128)} %collective-permute-done.3, f32[2,3,1,1024,512]{4,3,1,2,0:T(8,128)} %collective-permute-done.2, f32[1,3,1,1024,512]{4,3,1,2,0:T(8,128)} %copy-done.3, f32[1,3,1,1024,512]{4,3,1,2,0:T(8,128)} %copy-done.5, f32[1,3,1,1024,512]{4,3,1,2,0:T(8,128)} %copy-done.7, ...), kind=kLoop, calls=%fused_computation.127 | loop fusion | flops 18874368 | bytes 69206016 | tf_op jit(solution)/shard_map/sub | solution.py:46
  1481.9 12.2 maximum_select_fusion.2
  1494.2 16.1 fusion.3
  1510.3 15.0 fusion.2
  1525.3 21.4 %subtract_bitcast_fusion.1 = f32[1,3,1,1024,512]{4,3,1,2,0:T(8,128)S(1)} fusion(f32[3,1024,512]{2,1,0:T(8,128)} %fusion.3, f32[2,3,1,1024,512]{4,3,1,2,0:T(8,128)S(1)} %maximum_select_fusion.2, s32[512]{0:T(512)S(1)} %multiply_add_fusion.6), kind=kOutput, calls=%fused_computation.22 | convolution fusion | flops 9668919296 | bytes 18876416 | tf_op jit(solution)/shard_map/clyx,kx->clyk/dot_general | solution.py:72
  1546.7 16.7 add_bitcast_fusion.1
  1574.5 268.4 %collective-permute-done.4 = f32[2,3,1,1024,512]{4,3,1,2,0:T(8,128)} collective-permute-done((f32[2,3,1,1024,512]{4,3,1,2,0:T(8,128)}, f32[2,3,1,1024,512]{4,3,1,2,0:T(8,128)}, u32[]{:S(2)}, u32[]{:S(2)}) %collective-permute-start.4) | collective-permute-done | bytes 12582944 | tf_op jit(solution)/shard_map/ppermute | solution.py:29
  1843.0 14.5 fusion.83
  1870.2 14.0 maximum_select_fusion.3
  1887.5 19.1 collective-permute-done.5
  1906.6 22.8 %fusion.85 = f32[2,3,1,1024,512]{4,3,1,2,0:T(8,128)} fusion(f32[2,3,1,1024,512]{4,3,1,2,0:T(8,128)} %collective-permute-done.5, f32[2,3,1,1024,512]{4,3,1,2,0:T(8,128)} %collective-permute-done.4, f32[1,3,1,1024,512]{4,3,1,2,0:T(8,128)} %add_bitcast_fusion.1, f32[1,3,1,1024,512]{4,3,1,2,0:T(8,128)} %copy-done, f32[1,3,1,1024,512]{4,3,1,2,0:T(8,128)} %get-tuple-element.8, ...), kind=kLoop, calls=%fused_computation.125 | loop fusion | flops 15728640 | bytes 62914560 | tf_op jit(solution)/shard_map/sub | solution.py:46
  1937.8 25.1 %maximum_select_fusion.4 = f32[2,3,1,1024,512]{4,3,1,2,0:T(8,128)} fusion(f32[1,3,1,1024,512]{4,3,1,2,0:T(8,128)} %get-tuple-element.6, f32[1,3,1,1024,512]{4,3,1,2,0:T(8,128)} %get-tuple-element.5, f32[2,3,1,1024,512]{4,3,1,2,0:T(8,128)} %collective-permute-done.5, pred[]{:T(512)S(6)} %eq.19, f32[2,3,1,1024,512]{4,3,1,2,0:T(8,128)} %collective-permute-done.4, ...), kind=kLoop, calls=%fused_computation.8 | loop fusion | flops 22020096 | bytes 75497472 | tf_op jit(solution)/shard_map/jit(_where)/select_n | solution.py:57
  1962.9 40.3 %fusion.7 = f32[1024,3,512]{2,0,1:T(8,128)S(1)} fusion(f32[2,3,1,1024,512]{4,3,1,2,0:T(8,128)} %maximum_select_fusion.4, s32[1024]{0:T(1024)S(1)} %multiply_add_fusion.5), kind=kOutput, calls=%fused_computation.37 | convolution fusion | flops 19343081472 | bytes 12587008 | tf_op jit(solution)/shard_map/clyx,ky->clkx/dot_general | solution.py:91
  2003.2 38.6 %fusion.6 = f32[1024,3,512]{2,0,1:T(8,128)} fusion(f32[2,3,1,1024,512]{4,3,1,2,0:T(8,128)S(1)} %copy-done.10, s32[1024]{0:T(1024)S(1)} %multiply_add_fusion.5), kind=kOutput, calls=%fused_computation.36 | convolution fusion | flops 19342032896 | bytes 12587008 | tf_op jit(solution)/shard_map/clyx,ky->clkx/dot_general | solution.py:91
  2041.8 36.4 %subtract_bitcast_fusion = f32[1,3,1,1024,512]{4,3,1,2,0:T(8,128)S(1)} fusion(f32[1024,3,512]{2,0,1:T(8,128)S(1)} %fusion.7, f32[2,3,1,1024,512]{4,3,1,2,0:T(8,128)S(1)} %copy-done.10, s32[1024]{0:T(1024)S(1)} %multiply_add_fusion.5), kind=kOutput, calls=%fused_computation.16 | convolution fusion | flops 19343605760 | bytes 18878464 | tf_op jit(solution)/shard_map/clyx,ky->clkx/dot_general | solution.py:91
  2078.2 41.0 %add_bitcast_fusion = f32[1,3,1,1024,512]{4,3,1,2,0:T(8,128)} fusion(f32[1024,3,512]{2,0,1:T(8,128)} %fusion.6, f32[2,3,1,1024,512]{4,3,1,2,0:T(8,128)S(1)} %copy-done.10, s32[1024]{0:T(1024)S(1)} %multiply_add_fusion.5), kind=kOutput, calls=%fused_computation.15 | convolution fusion | flops 19344654336 | bytes 18878464 | tf_op jit(solution)/shard_map/clyx,ky->clkx/dot_general | solution.py:91
  (58 shorter events, 104.9 us)
Async XLA Ops:
  2.2 6.8 collective-permute-start
  572.2 272.6 %collective-permute-start.1 = (f32[1,3,1,1024,512]{4,3,1,2,0:T(8,128)}, f32[1,3,1,1024,512]{4,3,1,2,0:T(8,128)}, u32[]{:S(2)}, u32[]{:S(2)}) collective-permute-start(f32[1,3,1,1024,512]{4,3,1,2,0:T(8,128)} %maximum_multiply_fusion), channel_id=1, source_target_pairs={{0,16},{16,0},{4,20},{20,4},{8,24},{24,8},{12,28},{28,12},{1,17},{... | collective-permute-start | bytes 18874376 | tf_op jit(solution)/shard_map/ppermute | solution.py:29
  850.6 6.8 copy-start.3
  850.6 8.3 copy-start.5
  850.6 10.1 copy-start.7
  860.7 271.7 %collective-permute-start.2 = (f32[2,3,1,1024,512]{4,3,1,2,0:T(8,128)}, f32[2,3,1,1024,512]{4,3,1,2,0:T(8,128)}, u32[]{:S(2)}, u32[]{:S(2)}) collective-permute-start(f32[2,3,1,1024,512]{4,3,1,2,0:T(8,128)} %maximum_select_fusion), channel_id=1, source_target_pairs={{0,8},{8,0},{4,12},{12,4},{16,24},{24,16},{20,28},{28,20},{1,9},{9... | collective-permute-start | bytes 37748744 | tf_op jit(solution)/shard_map/ppermute | solution.py:29
  1149.0 10.3 copy-start.4
  1149.0 12.6 copy-start.6
  1149.0 14.4 copy-start.8
  1179.1 270.8 %collective-permute-start.3 = (f32[2,3,1,1024,512]{4,3,1,2,0:T(8,128)}, f32[2,3,1,1024,512]{4,3,1,2,0:T(8,128)}, u32[]{:S(2)}, u32[]{:S(2)}) collective-permute-start(f32[2,3,1,1024,512]{4,3,1,2,0:T(8,128)} %maximum_select_fusion.1), channel_id=1, source_target_pairs={{0,4},{4,0},{8,12},{12,8},{16,20},{20,16},{24,28},{28,24},{1,5},{5... | collective-permute-start | bytes 37748744 | tf_op jit(solution)/shard_map/ppermute | solution.py:29
  1546.7 16.7 copy-start
  1573.1 269.9 %collective-permute-start.4 = (f32[2,3,1,1024,512]{4,3,1,2,0:T(8,128)}, f32[2,3,1,1024,512]{4,3,1,2,0:T(8,128)}, u32[]{:S(2)}, u32[]{:S(2)}) collective-permute-start(f32[2,3,1,1024,512]{4,3,1,2,0:T(8,128)} %pad_maximum_fusion), channel_id=1, source_target_pairs={{0,2},{2,0},{1,3},{3,1},{4,6},{6,4},{5,7},{7,5},{8,10},{10,8},{9,1... | collective-permute-start | bytes 37748744 | tf_op jit(solution)/shard_map/ppermute | solution.py:29
  1857.4 9.6 copy-start.1
  1857.4 12.8 copy-start.2
  1864.8 19.5 copy-start.9
  1870.2 67.5 %slice-start = ((s8[6291456]{0:T(1024)(128)(4,1)}), s8[2097152]{0:T(1024)(128)(4,1)S(1)}, s32[]{:S(2)}) async-start(s8[6291456]{0:T(1024)(128)(4,1)} %bitcast.82), calls=%async_computation | async-start | bytes 4194304
  1884.3 22.3 %collective-permute-start.5 = (f32[2,3,1,1024,512]{4,3,1,2,0:T(8,128)}, f32[2,3,1,1024,512]{4,3,1,2,0:T(8,128)}, u32[]{:S(2)}, u32[]{:S(2)}) collective-permute-start(f32[2,3,1,1024,512]{4,3,1,2,0:T(8,128)} %maximum_select_fusion.3), channel_id=1, source_target_pairs={{0,1},{1,0},{2,3},{3,2},{4,5},{5,4},{6,7},{7,6},{8,9},{9,8},{10,11... | collective-permute-start | bytes 37748744 | tf_op jit(solution)/shard_map/ppermute | solution.py:29
  1887.5 50.3 %slice-start.1 = ((s8[6291456]{0:T(1024)(128)(4,1)}), s8[4194304]{0:T(1024)(128)(4,1)S(1)}, s32[]{:S(2)}) async-start(s8[6291456]{0:T(1024)(128)(4,1)} %bitcast.82), calls=%async_computation.1 | async-start | bytes 8388608
  1962.9 40.3 %copy-start.10 = (f32[2,3,1,1024,512]{4,3,1,2,0:T(8,128)S(1)}, f32[2,3,1,1024,512]{4,3,1,2,0:T(8,128)}, u32[]{:S(2)}) copy-start(f32[2,3,1,1024,512]{4,3,1,2,0:T(8,128)} %maximum_select_fusion.4) | copy-start | bytes 37748740
where the time goes:
time: 2130 us
  waiting for transfers between devices  1100 us (52%)
  other arithmetic  769 us (36%)
  matrix products  225 us (11%)
  local copies, waits for them, and re-layouts  21.5 us (1%)
    ppermute x5, waiting for transfers between devices, partner_2(): return lax.ppermute(block, axis, route)  1100 us
    scatter-add x3, other arithmetic, shards(): jax.ops.segment_sum(weights[component], cell_ids, num_segments=cell_total)  549 us
    dot_general x4, matrix products, product(): jnp.einsum('clyx,ky->clkx', data, table, precision=lax.Precision.HIGHEST,...  156 us
    sub x4, other arithmetic, section_mix(): difference = partner - parts  78.7 us
    select_n x5, other arithmetic, section_mix(): return jnp.where(upper_half, turned, summed)  73.8 us
    dot_general x4, matrix products, product(): jnp.einsum('clyx,kx->clyk', data, table, precision=lax.Precision.HIGHEST,...  69.2 us
  transfers between devices with their start and end apart: 6, of which 6 were waited for; matrix products, arithmetic and copies ran while one was open for 0% of the time, Pallas kernels for 0%

commit v1 on v0

--- a/solution.py
+++ b/solution.py
@@ -3,6 +3,8 @@
 import jax
 import jax.numpy as jnp
 from jax import lax
+from jax.experimental import pallas as pl
+from jax.experimental.pallas import tpu as pltpu
 from jax.sharding import PartitionSpec as P
 
 NX = 4096
@@ -11,12 +13,29 @@
 
 
 TWO_PI = 2.0 * math.pi
+
+BIN_ROWS = 256
+BIN_COLS = 32
+CHUNK = 256
+LANES = 128
 
 
 def from_behind(value, axis, steps):
     count = lax.axis_size(axis)
     pairs = [(source, (source + steps) % count) for source in range(count)]
     return lax.ppermute(value, axis, pairs)
+
+
+def flip(value, axis, mask):
+    count = lax.axis_size(axis)
+    return lax.ppermute(value, axis, [(source, source ^ mask) for source in range(count)])
+
+
+def bit_reverse(slab_index, bit_count):
+    result = jnp.zeros_like(slab_index)
+    for level in range(bit_count):
+        result = result | (slab_index >> level & 1) << bit_count - 1 - level
+    return result
 
 
 def partner_2(block, axis, stride):
@@ -27,13 +46,6 @@
         if high != low and high < count:
             route += [(low, high), (high, low)]
     return lax.ppermute(block, axis, route)
-
-
-def bit_reverse(slab_index, bit_count):
-    result = jnp.zeros_like(slab_index)
-    for level in range(bit_count):
-        result = result | (slab_index >> level & 1) << bit_count - 1 - level
-    return result
 
 
 def section_mix(parts, partner, slab_index, bit_number):
@@ -66,11 +78,10 @@
     return (jnp.cos(phase_angle), -jnp.sin(phase_angle))
 
 
-def along_columns(parts, table_real, table_imag):
-
+def along(parts, table_real, table_imag, spec):
     def product(data, table):
         return jnp.einsum(
-            "clyx,kx->clyk",
+            spec,
             data,
             table,
             precision=lax.Precision.HIGHEST,
@@ -85,26 +96,7 @@
     )
 
 
-def along_rows(parts, table_real, table_imag):
-
-    def product(data, table):
-        return jnp.einsum(
-            "clyx,ky->clkx",
-            data,
-            table,
-            precision=lax.Precision.HIGHEST,
-            preferred_element_type=jnp.float32,
-        )
-
-    return jnp.stack(
-        [
-            product(parts[0], table_real) - product(parts[1], table_imag),
-            product(parts[0], table_imag) + product(parts[1], table_real),
-        ]
-    )
-
-
-def shards(
+def dense_shards(
     resident_rows,
     resident_columns,
     resident_strength,
@@ -139,30 +131,379 @@
         ]
     )
     vorticity = deposited.reshape(1, 3, LEV, cells_y, cells_x) * (1.0 / math.sqrt(NX * NY))
-    bits_x = lax.axis_size("gx").bit_length() - 1
     parts = vorticity
-    slab_index = lax.axis_index("gx")
-    for bit_number in range(bits_x - 1, -1, -1):
-        partner = partner_2(parts, "gx", bit_number)
-        parts = section_mix(parts, partner, slab_index, bit_number)
-    table_real, table_imag = local_table(
-        bit_reverse(lax.axis_index("gx"), bits_x), lax.axis_size("gx"), cells_x
-    )
-    parts = along_columns(parts, table_real, table_imag)
-    bits_y = lax.axis_size("gy").bit_length() - 1
-    slab_index = lax.axis_index("gy")
-    for bit_number in range(bits_y - 1, -1, -1):
-        partner = partner_2(parts, "gy", bit_number)
-        parts = section_mix(parts, partner, slab_index, bit_number)
-    table_real, table_imag = local_table(
-        bit_reverse(lax.axis_index("gy"), bits_y), lax.axis_size("gy"), cells_y
-    )
-    return along_rows(parts, table_real, table_imag)
+    for axis, cells, spec in (
+        ("gx", cells_x, "clyx,kx->clyk"),
+        ("gy", cells_y, "clyx,ky->clkx"),
+    ):
+        bits = lax.axis_size(axis).bit_length() - 1
+        slab_index = lax.axis_index(axis)
+        for bit_number in range(bits - 1, -1, -1):
+            partner = partner_2(parts, axis, bit_number)
+            parts = section_mix(parts, partner, slab_index, bit_number)
+        table_real, table_imag = local_table(bit_reverse(slab_index, bits), 1 << bits, cells)
+        parts = along(parts, table_real, table_imag, spec)
+    return parts
+
+
+def bin_key(rows, columns, cells_x):
+    column = (columns & 1) * (cells_x // 2) + (columns >> 1)
+    bin_index = (column // BIN_COLS) * 4 + (rows & 3)
+    return bin_index * (BIN_ROWS * BIN_COLS) + (rows >> 2) * BIN_COLS + column % BIN_COLS
+
+
+def deposit(sources, signs, cells_x, cells_y):
+    count = len(sources)
+    row_bins = cells_y // BIN_ROWS
+    col_bins = cells_x // BIN_COLS
+    bins = row_bins * col_bins
+    width = sources[0].shape[-1]
+    first_start = width - LANES
+    shift = BIN_COLS.bit_length() - 1
+    starts = jnp.stack(
+        [source[0, first_start : first_start + bins + 1] for source in sources]
+    ).astype(jnp.int32)
+
+    def kernel(starts_ref, signs_ref, *refs):
+        source_refs, out_ref = refs[:count], refs[count]
+        group = pl.program_id(0)
+        spans = []
+        steps = jnp.int32(0)
+        for row_bin in range(row_bins):
+            bin_index = group * row_bins + row_bin
+            for s in range(count):
+                begin = starts_ref[s, bin_index]
+                end = starts_ref[s, bin_index + 1]
+                aligned = (begin // LANES) * LANES
+                spans.append((aligned, begin, end))
+                steps = jnp.maximum(steps, (end - aligned + CHUNK - 1) // CHUNK)
+        lane = lax.broadcasted_iota(jnp.int32, (1, CHUNK), 1)
+
+        def ramp(length):
+            return (
+                lax.broadcasted_iota(jnp.int32, (length, CHUNK), 0)
+                .astype(jnp.float32)
+                .astype(jnp.bfloat16)
+            )
+
+        row_ramp, col_ramp = ramp(BIN_ROWS), ramp(BIN_COLS)
+        one, zero = jnp.bfloat16(1), jnp.bfloat16(0)
+
+        def body(step, carry):
+            totals = []
+            for row_bin in range(row_bins):
+                base = (group * row_bins + row_bin) * (BIN_ROWS * BIN_COLS)
+                hits, weights = [], []
+                for s in range(count):
+                    aligned, begin, end = spans[row_bin * count + s]
+                    here = aligned + step * CHUNK
+                    offset = pl.multiple_of(jnp.minimum(here, width - CHUNK), LANES)
+                    block = source_refs[s][:, pl.ds(offset, CHUNK)]
+                    place = lane + offset
+                    valid = (place >= jnp.maximum(begin, here)) & (place < end)
+                    local = block[0:1].astype(jnp.int32) - base
+                    row = jnp.where(valid, lax.shift_right_arithmetic(local, shift), -1)
+                    col = local & (BIN_COLS - 1)
+                    row = row.astype(jnp.float32).astype(jnp.bfloat16)
+                    col = col.astype(jnp.float32).astype(jnp.bfloat16)
+                    hits.append(jnp.where(row_ramp == row, one, zero))
+                    mask = col_ramp == col
+                    value = block * signs_ref[s]
+                    high = value.astype(jnp.bfloat16)
+                    low = (value - high.astype(jnp.float32)).astype(jnp.bfloat16)
+                    weights.append(
+                        jnp.concatenate(
+                            [
+                                jnp.where(
+                                    mask,
+                                    jnp.broadcast_to(piece[k : k + 1], (BIN_COLS, CHUNK)),
+                                    zero,
+                                )
+                                for piece in (high, low)
+                                for k in (1, 2, 3)
+                            ],
+                            axis=0,
+                        )
+                    )
+                total = lax.dot_general(
+                    jnp.concatenate(weights, axis=1),
+                    jnp.concatenate(hits, axis=1),
+                    (((1,), (1,)), ((), ())),
+                    preferred_element_type=jnp.float32,
+                )
+                totals.append(total[: 3 * BIN_COLS] + total[3 * BIN_COLS :])
+            for row_bin in range(row_bins):
+                where = slice(row_bin * BIN_ROWS, (row_bin + 1) * BIN_ROWS)
+                out_ref[:, :, where] += totals[row_bin].reshape(3, BIN_COLS, BIN_ROWS)
+            return carry
+
+        out_ref[...] = jnp.zeros_like(out_ref)
+        lax.fori_loop(0, steps, body, 0)
+
+    flops = count * width * BIN_ROWS * BIN_COLS * 12
+    return pl.pallas_call(
+        kernel,
+        grid_spec=pltpu.PrefetchScalarGridSpec(
+            num_scalar_prefetch=1,
+            grid=(col_bins,),
+            in_specs=[pl.BlockSpec(memory_space=pltpu.SMEM)]
+            + [pl.BlockSpec(memory_space=pltpu.VMEM)] * count,
+            out_specs=pl.BlockSpec((3, BIN_COLS, cells_y), lambda g, starts: (0, g, 0)),
+        ),
+        out_shape=jax.ShapeDtypeStruct((3, cells_x, cells_y), jnp.float32),
+        compiler_params=pltpu.CompilerParams(vmem_limit_bytes=40 << 20),
+        cost_estimate=pl.CostEstimate(
+            flops=flops * 2, bytes_accessed=12 * cells_x * cells_y, transcendentals=0
+        ),
+        name="deposit",
+    )(starts, signs, *sources)
+
+
+def turns(numerator, total):
+    angle = (numerator % total).astype(jnp.float32) * (TWO_PI / total)
+    return jnp.cos(angle), -jnp.sin(angle)
+
+
+def stage_table(k_first, slab_count, radix, length):
+    total = slab_count * radix * length
+    shape = (radix, length, length)
+    residue = lax.broadcasted_iota(jnp.int32, shape, 0)
+    k = k_first + slab_count * lax.broadcasted_iota(jnp.int32, shape, 1)
+    n = radix * lax.broadcasted_iota(jnp.int32, shape, 2) + residue
+    real, imag = turns(k * n, total)
+    return jnp.concatenate(
+        [jnp.concatenate([real, -imag], axis=2), jnp.concatenate([imag, real], axis=2)], axis=1
+    )
+
+
+def split(value):
+    high = value.astype(jnp.bfloat16)
+    return high, (value - high.astype(jnp.float32)).astype(jnp.bfloat16)
+
+
+def fill_tables(table_ref, held_ref, radix):
+    for residue in range(radix):
+        high, low = split(table_ref[residue])
+        held_ref[residue] = jnp.concatenate([high, high, low], axis=1)
+
+
+def columns_transform(meshes, scalars, table, component, block):
+    count = len(meshes)
+    cells_x, cells_y = meshes[0].shape[1:]
+    half = cells_x // 2
+
+    def kernel(scalars_ref, table_ref, *refs):
+        mesh_refs, out_ref, held_ref = refs[:count], refs[count], refs[count + 1]
+
+        @pl.when(pl.program_id(0) == 0)
+        def _():
+            fill_tables(table_ref, held_ref, 2)
+
+        pieces = []
+        for residue in range(2):
+            rows = slice(residue * half, (residue + 1) * half)
+            data = [mesh_ref[0, rows, :] for mesh_ref in mesh_refs]
+            real = sum(scalars_ref[0, i] * data[i] for i in range(count))
+            imag = sum(scalars_ref[1, i] * data[i] for i in range(count))
+            high, low = split(jnp.concatenate([real, imag], axis=0))
+            pieces.append(
+                jnp.dot(
+                    held_ref[residue],
+                    jnp.concatenate([high, low, high], axis=0),
+                    preferred_element_type=jnp.float32,
+                )
+            )
+        for part in range(2):
+            rows = slice(part * half, (part + 1) * half)
+            out_ref[part, 0, :half] = pieces[0][rows] + pieces[1][rows]
+            out_ref[part, 0, half:] = pieces[0][rows] - pieces[1][rows]
+
+    return pl.pallas_call(
+        kernel,
+        grid=(cells_y // block,),
+        in_specs=[
+            pl.BlockSpec(memory_space=pltpu.SMEM),
+            pl.BlockSpec(memory_space=pltpu.VMEM),
+        ]
+        + [pl.BlockSpec((1, cells_x, block), lambda g: (component, 0, g))] * count,
+        out_specs=pl.BlockSpec((2, 1, cells_x, block), lambda g: (0, 0, 0, g)),
+        out_shape=jax.ShapeDtypeStruct((2, 1, cells_x, cells_y), jnp.float32),
+        scratch_shapes=[pltpu.VMEM((2, cells_x, 3 * cells_x), jnp.bfloat16)],
+        compiler_params=pltpu.CompilerParams(vmem_limit_bytes=40 << 20),
+        cost_estimate=pl.CostEstimate(
+            flops=12 * cells_x * cells_x * cells_y,
+            bytes_accessed=(count + 2) * 4 * cells_x * cells_y,
+            transcendentals=0,
+        ),
+        name="columns_transform",
+    )(scalars, table, *meshes)
+
+
+def rows_transform(owns, partners, scalars, table, block):
+    count = len(owns)
+    cells_x, cells_y = owns[0].shape[2:]
+    quarter = cells_y // 4
+
+    def kernel(scalars_ref, table_ref, *refs):
+        own_refs, partner_refs = refs[:count], refs[count : 2 * count]
+        out_ref, held_ref = refs[2 * count :]
+
+        @pl.when(pl.program_id(0) == 0)
+        def _():
+            fill_tables(table_ref, held_ref, 4)
+
+        own_real, own_imag = scalars_ref[0], scalars_ref[1]
+        other_real, other_imag = scalars_ref[2], scalars_ref[3]
+        for c in range(count):
+            pieces = []
+            for residue in range(4):
+                where = slice(residue * quarter, (residue + 1) * quarter)
+                a, b = own_refs[c][0, 0, :, where], own_refs[c][1, 0, :, where]
+                d, e = partner_refs[c][0, 0, :, where], partner_refs[c][1, 0, :, where]
+                real = own_real * a - own_imag * b + other_real * d - other_imag * e
+                imag = own_real * b + own_imag * a + other_real * e + other_imag * d
+                high, low = split(jnp.concatenate([real, imag], axis=1))
+                piece = lax.dot_general(
+                    held_ref[residue],
+                    jnp.concatenate([high, low, high], axis=1),
+                    (((1,), (1,)), ((), ())),
+                    preferred_element_type=jnp.float32,
+                )
+                pieces.append((piece[:quarter], piece[quarter:]))
+            (ar, ai), (br, bi), (cr, ci), (dr, di) = pieces
+            even_r, even_i, odd_r, odd_i = ar + cr, ai + ci, br + dr, bi + di
+            diff_r, diff_i, turn_r, turn_i = ar - cr, ai - ci, br - dr, bi - di
+            out_ref[0, c, 0, 0 * quarter : 1 * quarter] = even_r + odd_r
+            out_ref[1, c, 0, 0 * quarter : 1 * quarter] = even_i + odd_i
+            out_ref[0, c, 0, 1 * quarter : 2 * quarter] = diff_r + turn_i
+            out_ref[1, c, 0, 1 * quarter : 2 * quarter] = diff_i - turn_r
+            out_ref[0, c, 0, 2 * quarter : 3 * quarter] = even_r - odd_r
+            out_ref[1, c, 0, 2 * quarter : 3 * quarter] = even_i - odd_i
+            out_ref[0, c, 0, 3 * quarter : 4 * quarter] = diff_r - turn_i
+            out_ref[1, c, 0, 3 * quarter : 4 * quarter] = diff_i + turn_r
+
+    spec = pl.BlockSpec((2, 1, block, cells_y), lambda g: (0, 0, g, 0))
+    return pl.pallas_call(
+        kernel,
+        grid=(cells_x // block,),
+        in_specs=[
+            pl.BlockSpec(memory_space=pltpu.SMEM),
+            pl.BlockSpec(memory_space=pltpu.VMEM),
+        ]
+        + [spec] * (2 * count),
+        out_specs=pl.BlockSpec((2, count, 1, cells_y, block), lambda g: (0, 0, 0, 0, g)),
+        out_shape=jax.ShapeDtypeStruct((2, count, 1, cells_y, cells_x), jnp.float32),
+        scratch_shapes=[pltpu.VMEM((4, 2 * quarter, 6 * quarter), jnp.bfloat16)],
+        compiler_params=pltpu.CompilerParams(vmem_limit_bytes=52 << 20),
+        cost_estimate=pl.CostEstimate(
+            flops=count * 6 * cells_y * cells_y * cells_x,
+            bytes_accessed=count * 24 * cells_x * cells_y,
+            transcendentals=0,
+        ),
+        name="rows_transform",
+    )(scalars, table, *owns, *partners)
+
+
+def particle_shards(
+    resident_rows,
+    resident_columns,
+    resident_strength,
+    crossing_rows,
+    crossing_columns,
+    crossing_strength,
+    crossing_count,
+):
+    cells_x = NX // lax.axis_size("gx")
+    cells_y = NY // lax.axis_size("gy")
+    bins = (cells_y // BIN_ROWS) * (cells_x // BIN_COLS)
+    gx, gy = lax.axis_index("gx"), lax.axis_index("gy")
+    x, z = gx & 1, gx >> 1
+    core, y = gy & 1, gy >> 1
+    kx_first = bit_reverse(gx, 3)
+    ky_first = bit_reverse(gy, 2)
+
+    slot_count = crossing_rows.shape[-1]
+    slot_index = lax.broadcasted_iota(jnp.int32, (1, slot_count), 1)
+    live_slot = (slot_index < crossing_count).astype(jnp.float32)
+    crossing_key = bin_key(crossing_rows.reshape(1, -1), crossing_columns.reshape(1, -1), cells_x)
+    outgoing = jnp.concatenate(
+        [crossing_key.astype(jnp.float32), crossing_strength.reshape(3, slot_count) * live_slot]
+    )
+    arrived = from_behind(outgoing, "gx", 1)
+    resident_key = bin_key(resident_rows.reshape(-1), resident_columns.reshape(-1), cells_x)
+    key = jnp.concatenate([resident_key, arrived[0].astype(jnp.int32)])
+    strength = [
+        jnp.concatenate([resident_strength[i].reshape(-1), arrived[1 + i]]) for i in range(3)
+    ]
+    key, *strength = lax.sort((key, *strength), num_keys=1, is_stable=False)
+    bounds = lax.broadcasted_iota(jnp.int32, (LANES, 1), 0) * (BIN_ROWS * BIN_COLS)
+    starts = jnp.sum((key[None, :] < bounds).astype(jnp.int32), axis=1)
+    particles = jnp.concatenate(
+        [
+            jnp.stack([key.astype(jnp.float32), *strength]),
+            jnp.concatenate([starts.astype(jnp.float32)[None], jnp.zeros((3, LANES), jnp.float32)]),
+        ],
+        axis=1,
+    )
+
+    near = {0: particles}
+    far = {0: flip(particles, "gy", 2)}
+    near[4] = flip(near[0], "gx", 4)
+    far[4] = flip(near[4], "gy", 2)
+    near[1] = flip(near[0], "gx", 1)
+    far[1] = flip(far[0], "gx", 1)
+    near[5] = flip(near[4], "gx", 1)
+    far[5] = flip(near[5], "gy", 2)
+    near[2] = flip(near[0], "gx", 2)
+    far[2] = flip(far[0], "gx", 2)
+    near[6] = flip(near[0], "gx", 6)
+    far[6] = flip(near[6], "gy", 2)
+    near[3] = flip(near[2], "gx", 1)
+    far[3] = flip(near[3], "gy", 2)
+    near[7] = flip(near[6], "gx", 1)
+    far[7] = flip(far[6], "gx", 1)
+
+    meshes, scalars = [], []
+    kx_low = kx_first & 3
+    for k in (0, 1, 2, 3):
+        slab_x = x ^ (k & 1)
+        slab_z = z ^ (k >> 1)
+        signs = []
+        for top in (0, 2):
+            for slab_y in (y, 1 - y):
+                flips = kx_low * ((slab_z ^ top) >> 1) + y * slab_y
+                signs.append((1 - 2 * (flips & 1)).astype(jnp.float32))
+        meshes.append(
+            deposit(
+                [near[k], far[k], near[k ^ 4], far[k ^ 4]], jnp.stack(signs), cells_x, cells_y
+            )
+        )
+        real, imag = turns(kx_first * slab_x + 2 * kx_low * (slab_z & 1), 8)
+        scalars.append(jnp.stack([real, imag]) * (1.0 / math.sqrt(NX * NY)))
+    scalars = jnp.stack(scalars, axis=1)
+
+    table = stage_table(kx_first, 8, 2, cells_x // 2)
+    owns = [columns_transform(meshes, scalars, table, i, 256) for i in range(3)]
+    partners = [flip(own, "gy", 1) for own in owns]
+
+    turn_real, turn_imag = turns(ky_first, 4)
+    low = core == 0
+    scalars = jnp.stack(
+        [
+            jnp.where(low, 1.0, turn_real),
+            jnp.where(low, 0.0, turn_imag),
+            jnp.where(low, turn_real, 1.0),
+            jnp.where(low, turn_imag, 0.0),
+        ]
+    )
+    table = stage_table(ky_first, 4, 4, cells_y // 4)
+    return rows_transform(owns, partners, scalars, table, 128)
 
 
 def solution(mesh):
+    few = mesh.shape["gx"] == 8 and mesh.shape["gy"] == 4
     return jax.shard_map(
-        shards,
+        particle_shards if few else dense_shards,
         mesh=mesh,
         in_specs=(
             P("gy", "gx", None),

time: 2130 us -> 386 us (0.18)
  waiting for transfers between devices: 1100 us -> 61.3 us
  other arithmetic: 769 us -> 53.5 us
  Pallas kernels: 0 us -> 234 us
  matrix products: 225 us -> 0 us
    ppermute x5 -> x18, waiting for transfers between devices: 1100 us -> 60.3 us  [flip(): lax.ppermute(value, axis, [(source, source ^ mask) for source in range(co...]
    scatter-add x3 -> x0, other arithmetic: 549 us -> none  [shards(): jax.ops.segment_sum(weights[component], cell_ids, num_segments=cell_total)]
    pallas_call x0 -> x8, Pallas kernels: none -> 234 us  [the longest x4 183 us: deposit(): pl.pallas_call(kernel, grid_spec=pltpu.PrefetchScalarGridSpec(num_scalar_...]
    dot_general x8 -> x0, matrix products: 225 us -> none  [the longest x4 156 us: product(): jnp.einsum('clyx,ky->clkx', data, table, precision=lax.Precision.HIGHEST,...]
    sub x8 -> x0, other arithmetic: 112 us -> none  [the longest x4 78.7 us: section_mix(): difference = partner - parts]
    select_n x5 -> x0, other arithmetic: 73.8 us -> none  [section_mix(): return jnp.where(upper_half, turned, summed)]
    sort x0 -> x1, other arithmetic: none -> 37.2 us  [particle_shards(): key, *strength = lax.sort((key, *strength), num_keys=1, is_stable=False)]
  transfers between devices with their start and end apart: 6 -> 19, of which waited for: 6 -> 7; matrix products, arithmetic and copies ran while one was open for 0% -> 3% of each run, Pallas kernels for 0% -> 24%
where the time goes in v1:
time: 386 us; the launch traced here: 379 us
  Pallas kernels  234 us (61%)
  waiting for transfers between devices  61.3 us (16%)
  other arithmetic  53.5 us (14%)
  starting transfers between devices  19.3 us (5%)
  local copies, waits for them, and re-layouts  9.04 us (2%)
    pallas_call x4, Pallas kernels, deposit(): pl.pallas_call(kernel, grid_spec=pltpu.PrefetchScalarGridSpec(num_scalar_...  183 us
    ppermute x18, waiting for transfers between devices, flip(): lax.ppermute(value, axis, [(source, source ^ mask) for source in range(co...  60.3 us
    sort x1, other arithmetic, particle_shards(): key, *strength = lax.sort((key, *strength), num_keys=1, is_stable=False)  37.2 us
    pallas_call x1, Pallas kernels, rows_transform(): pl.pallas_call(kernel, grid=(cells_x // block,), in_specs=[pl.BlockSpec(m...  27 us
    pallas_call x3, Pallas kernels, columns_transform(): pl.pallas_call(kernel, grid=(cells_y // block,), in_specs=[pl.BlockSpec(m...  24.2 us
    ppermute x18, starting transfers between devices, flip(): lax.ppermute(value, axis, [(source, source ^ mask) for source in range(co...  17.2 us
    unnamed x6, local copies, waits for them, and re-layouts  7.95 us
  transfers between devices with their start and end apart: 19, of which 7 were waited for; matrix products, arithmetic and copies ran while one was open for 3% of the time, Pallas kernels for 24%

profile of v1, /device:TPU:1, one launch (start us, length us, event | category | flops | bytes accessed | tf_op | source)
XLA Modules:
  0.0 379.5 jit_solution(14194335548481441085)
XLA Ops:
  8.8 37.2 %sort.27 = (s32[34816]{0:T(1024)S(1)}, f32[34816]{0:T(1024)S(1)}, f32[34816]{0:T(1024)S(1)}, f32[34816]{0:T(1024)S(1)}) sort(s32[34816]{0:T(1024)S(1)} %pad_add_fusion, f32[34816]{0:T(1024)S(1)} %get-tuple-element.36, f32[34816]{0:T(1024)S(1)} %get-tuple-element.37, f32[34816]{0:T(1024)S(1)} %pad_maximum_fusion.2), dimensions={0}, to_apply=%region_0.1 | sort | flops 557056 | bytes 1114112 | tf_op jit(solution)/shard_map/sort | solution.py:438
  48.6 2.5 collective-permute-start.10
  54.6 2.1 fusion.9
  56.8 6.5 %collective-permute-done.10.refs_2_ = f32[4,34944]{1,0:T(4,128)S(1)} collective-permute-done((f32[4,34944]{1,0:T(4,128)S(1)}, f32[4,34944]{1,0:T(4,128)S(1)}, u32[]{:S(2)}, u32[]{:S(2)}) %collective-permute-start.10) | collective-permute-done | bytes 559136 | tf_op jit(solution)/shard_map/ppermute | solution.py:31
  64.3 14.3 %collective-permute-done.8.refs_0_ = f32[4,34944]{1,0:T(4,128)S(1)} collective-permute-done((f32[4,34944]{1,0:T(4,128)S(1)}, f32[4,34944]{1,0:T(4,128)S(1)}, u32[]{:S(2)}, u32[]{:S(2)}) %collective-permute-start.8) | collective-permute-done | bytes 559136 | tf_op jit(solution)/shard_map/ppermute | solution.py:31
  78.6 19.3 %collective-permute-done.2.refs_2_ = f32[4,34944]{1,0:T(4,128)S(1)} collective-permute-done((f32[4,34944]{1,0:T(4,128)S(1)}, f32[4,34944]{1,0:T(4,128)S(1)}, u32[]{:S(2)}, u32[]{:S(2)}) %collective-permute-start.2) | collective-permute-done | bytes 559136 | tf_op jit(solution)/shard_map/ppermute | solution.py:31
  101.7 8.5 %collective-permute-done.3.refs_3_ = f32[4,34944]{1,0:T(4,128)S(1)} collective-permute-done((f32[4,34944]{1,0:T(4,128)S(1)}, f32[4,34944]{1,0:T(4,128)S(1)}, u32[]{:S(2)}, u32[]{:S(2)}) %collective-permute-start.3) | collective-permute-done | bytes 559136 | tf_op jit(solution)/shard_map/ppermute | solution.py:31
  110.3 2.3 collective-permute-start.5
  114.5 45.7 %deposit.4.refs_0_ = f32[3,512,1024]{2,1,0:T(8,128)S(1)} custom-call(s32[4,65]{1,0:T(4,128)S(1)} %maximum_convert_fusion.starts_ref, f32[4]{0:T(128)S(1)} %pad_maximum_fusion.6.signs_ref, f32[4,34944]{1,0:T(4,128)S(1)} %select_maximum_fusion.refs_0_, f32[4,34944]{1,0:T(4,128)S(1)} %collective-permute-done.1.refs_1_, ...), custom_call_target="tpu_custom_call" | custom-call | flops 27481079808 | bytes 6291456 | tf_op jit(solution)/shard_map/deposit/pallas_call | solution.py:244
  160.2 45.7 %deposit.6.refs_2_ = f32[3,512,1024]{2,1,0:T(8,128)S(1)} custom-call(s32[4,65]{1,0:T(4,128)S(1)} %maximum_convert_fusion.2.starts_ref, f32[4]{0:T(128)S(1)} %pad_maximum_fusion.7.signs_ref, f32[4,34944]{1,0:T(4,128)S(1)} %collective-permute-done.8.refs_0_, f32[4,34944]{1,0:T(4,128)S(1)} %collective-permute-done.9.refs_1_, ...), custom_call_target="tpu_custom_call" | custom-call | flops 27481079808 | bytes 6291456 | tf_op jit(solution)/shard_map/deposit/pallas_call | solution.py:244
  205.9 2.7 copy-done
  208.7 45.7 %deposit.5.refs_1_ = f32[3,512,1024]{2,1,0:T(8,128)S(1)} custom-call(s32[4,65]{1,0:T(4,128)S(1)} %maximum_convert_fusion.1.starts_ref, f32[4]{0:T(128)S(1)} %pad_maximum_fusion.6.signs_ref, f32[4,34944]{1,0:T(4,128)S(1)} %collective-permute-done.4.refs_0_, f32[4,34944]{1,0:T(4,128)S(1)} %collective-permute-done.5.refs_1_, ...), custom_call_target="tpu_custom_call" | custom-call | flops 27481079808 | bytes 6291456 | tf_op jit(solution)/shard_map/deposit/pallas_call | solution.py:244
  254.5 2.7 copy-done.1
  257.2 45.7 %deposit.7.refs_3_ = f32[3,512,1024]{2,1,0:T(8,128)S(1)} custom-call(s32[4,65]{1,0:T(4,128)S(1)} %maximum_convert_fusion.3.starts_ref, f32[4]{0:T(128)S(1)} %pad_maximum_fusion.7.signs_ref, f32[4,34944]{1,0:T(4,128)S(1)} %collective-permute-done.12.refs_0_, f32[4,34944]{1,0:T(4,128)S(1)} %collective-permute-done.13.refs_1_, ...), custom_call_target="tpu_custom_call" | custom-call | flops 27481079808 | bytes 6291456 | tf_op jit(solution)/shard_map/deposit/pallas_call | solution.py:244
  302.9 2.6 copy-done.2
  305.5 8.0 %columns_transform.5.refs_2_ = f32[2,1,512,1024]{3,2,1,0:T(8,128)} custom-call(f32[2,4]{1,0:T(2,128)S(1)} %pad_maximum_fusion.4.scalars_ref, f32[2,512,512]{2,1,0:T(8,128)S(1)} %maximum_maximum_fusion.1.table_ref, f32[3,512,1024]{2,1,0:T(8,128)S(1)} %deposit.4.refs_0_, f32[3,512,1024]{2,1,0:T(8,128)} %copy-done.1, f32[3,512,1024]{2,1,0:T(8,128)} %copy-done, ...), custom_call_target="tpu_custom_call" | custom-call | flops 3221225472 | bytes 12582912 | tf_op jit(solution)/shard_map/columns_transform/pallas_call | solution.py:321
  313.5 8.0 %columns_transform.4.refs_1_ = f32[2,1,512,1024]{3,2,1,0:T(8,128)} custom-call(f32[2,4]{1,0:T(2,128)S(1)} %pad_maximum_fusion.4.scalars_ref, f32[2,512,512]{2,1,0:T(8,128)S(1)} %maximum_maximum_fusion.1.table_ref, f32[3,512,1024]{2,1,0:T(8,128)S(1)} %deposit.4.refs_0_, f32[3,512,1024]{2,1,0:T(8,128)} %copy-done.1, f32[3,512,1024]{2,1,0:T(8,128)} %copy-done, ...), custom_call_target="tpu_custom_call" | custom-call | flops 3221225472 | bytes 12582912 | tf_op jit(solution)/shard_map/columns_transform/pallas_call | solution.py:321
  321.5 8.2 %columns_transform.3.refs_0_ = f32[2,1,512,1024]{3,2,1,0:T(8,128)} custom-call(f32[2,4]{1,0:T(2,128)S(1)} %pad_maximum_fusion.4.scalars_ref, f32[2,512,512]{2,1,0:T(8,128)S(1)} %maximum_maximum_fusion.1.table_ref, f32[3,512,1024]{2,1,0:T(8,128)S(1)} %deposit.4.refs_0_, f32[3,512,1024]{2,1,0:T(8,128)} %copy-done.1, f32[3,512,1024]{2,1,0:T(8,128)} %copy-done, ...), custom_call_target="tpu_custom_call" | custom-call | flops 3221225472 | bytes 12582912 | tf_op jit(solution)/shard_map/columns_transform/pallas_call | solution.py:321
  329.7 3.2 collective-permute-start.16
  333.7 4.2 %fusion.3 = (f32[4,256,256]{2,1,0:T(8,128)S(1)}, f32[4,256,256]{2,1,0:T(8,128)S(1)}, f32[4,256,256]{2,1,0:T(8,128)S(1)}) fusion(s32[256]{0:T(256)S(1)} %get-tuple-element.28, s32[256]{0:T(256)S(1)} %get-tuple-element.29), kind=kLoop, calls=%fused_computation.12 | loop fusion | flops 4194304 | bytes 3147776 | tf_op jit(solution)/shard_map/sin | solution.py:264
  337.9 2.5 maximum_maximum_fusion.table_ref
  340.4 5.7 %collective-permute-done.17.refs_4_ = f32[2,1,512,1024]{3,2,1,0:T(8,128)} collective-permute-done((f32[2,1,512,1024]{3,2,1,0:T(8,128)}, f32[2,1,512,1024]{3,2,1,0:T(8,128)}, u32[]{:S(2)}, u32[]{:S(2)}) %collective-permute-start.17) | collective-permute-done | bytes 4194336 | tf_op jit(solution)/shard_map/ppermute | solution.py:31
  346.1 6.0 %collective-permute-done.18.refs_5_ = f32[2,1,512,1024]{3,2,1,0:T(8,128)} collective-permute-done((f32[2,1,512,1024]{3,2,1,0:T(8,128)}, f32[2,1,512,1024]{3,2,1,0:T(8,128)}, u32[]{:S(2)}, u32[]{:S(2)}) %collective-permute-start.18) | collective-permute-done | bytes 4194336 | tf_op jit(solution)/shard_map/ppermute | solution.py:31
  352.1 27.0 %rows_transform.1 = f32[2,3,1,1024,512]{4,3,2,1,0:T(8,128)} custom-call(f32[4]{0:T(128)S(1)} %pad_maximum_fusion.5.scalars_ref, f32[4,512,512]{2,1,0:T(8,128)} %maximum_maximum_fusion.table_ref, f32[2,1,512,1024]{3,2,1,0:T(8,128)} %columns_transform.3.refs_0_, f32[2,1,512,1024]{3,2,1,0:T(8,128)} %columns_transform.4.refs_1_, ...), custom_call_target="tpu_custom_call" | custom-call | flops 9663676416 | bytes 37748736 | tf_op jit(solution)/shard_map/rows_transform/pallas_call | solution.py:386
  (77 shorter events, 20.8 us)
Async XLA Ops:
  2.3 6.4 %collective-permute-start = (f32[4,2048]{1,0:T(4,128)S(1)}, f32[4,2048]{1,0:T(4,128)S(1)}, u32[]{:S(2)}, u32[]{:S(2)}) collective-permute-start(f32[4,2048]{1,0:T(4,128)S(1)} %pad_maximum_fusion.3), channel_id=1, source_target_pairs={{0,4},{4,8},{8,12},{12,16},{16,20},{20,24},{24,28},{28,0},{1,5},{5... | collective-permute-start | bytes 98312 | tf_op jit(solution)/shard_map/ppermute | solution.py:26
  48.6 14.6 %collective-permute-start.10 = (f32[4,34944]{1,0:T(4,128)S(1)}, f32[4,34944]{1,0:T(4,128)S(1)}, u32[]{:S(2)}, u32[]{:S(2)}) collective-permute-start(f32[4,34944]{1,0:T(4,128)S(1)} %select_maximum_fusion.refs_0_), channel_id=1, source_target_pairs={{0,24},{4,28},{8,16},{12,20},{16,8},{20,12},{24,0},{28,4},{1,25},{... | collective-permute-start | bytes 1677320 | tf_op jit(solution)/shard_map/ppermute | solution.py:31
  51.1 27.5 %collective-permute-start.8 = (f32[4,34944]{1,0:T(4,128)S(1)}, f32[4,34944]{1,0:T(4,128)S(1)}, u32[]{:S(2)}, u32[]{:S(2)}) collective-permute-start(f32[4,34944]{1,0:T(4,128)S(1)} %select_maximum_fusion.refs_0_), channel_id=1, source_target_pairs={{0,8},{4,12},{8,0},{12,4},{16,24},{20,28},{24,16},{28,20},{1,9},{5... | collective-permute-start | bytes 1677320 | tf_op jit(solution)/shard_map/ppermute | solution.py:31
  51.1 46.9 %collective-permute-start.2 = (f32[4,34944]{1,0:T(4,128)S(1)}, f32[4,34944]{1,0:T(4,128)S(1)}, u32[]{:S(2)}, u32[]{:S(2)}) collective-permute-start(f32[4,34944]{1,0:T(4,128)S(1)} %select_maximum_fusion.refs_0_), channel_id=1, source_target_pairs={{0,16},{4,20},{8,24},{12,28},{16,0},{20,4},{24,8},{28,12},{1,17},{... | collective-permute-start | bytes 1677320 | tf_op jit(solution)/shard_map/ppermute | solution.py:31
  52.2 47.0 %collective-permute-start.1 = (f32[4,34944]{1,0:T(4,128)S(1)}, f32[4,34944]{1,0:T(4,128)S(1)}, u32[]{:S(2)}, u32[]{:S(2)}) collective-permute-start(f32[4,34944]{1,0:T(4,128)S(1)} %select_maximum_fusion.refs_0_), channel_id=1, source_target_pairs={{0,2},{1,3},{2,0},{3,1},{4,6},{5,7},{6,4},{7,5},{8,10},{9,11},{10,... | collective-permute-start | bytes 1677320 | tf_op jit(solution)/shard_map/ppermute | solution.py:31
  54.2 45.1 %collective-permute-start.4 = (f32[4,34944]{1,0:T(4,128)S(1)}, f32[4,34944]{1,0:T(4,128)S(1)}, u32[]{:S(2)}, u32[]{:S(2)}) collective-permute-start(f32[4,34944]{1,0:T(4,128)S(1)} %select_maximum_fusion.refs_0_), channel_id=1, source_target_pairs={{0,4},{4,0},{8,12},{12,8},{16,20},{20,16},{24,28},{28,24},{1,5},{5... | collective-permute-start | bytes 1677320 | tf_op jit(solution)/shard_map/ppermute | solution.py:31
  63.2 38.4 %collective-permute-start.11 = (f32[4,34944]{1,0:T(4,128)S(1)}, f32[4,34944]{1,0:T(4,128)S(1)}, u32[]{:S(2)}, u32[]{:S(2)}) collective-permute-start(f32[4,34944]{1,0:T(4,128)S(1)} %collective-permute-done.10.refs_2_), channel_id=1, source_target_pairs={{0,2},{1,3},{2,0},{3,1},{4,6},{5,7},{6,4},{7,5},{8,10},{9,11},{10,... | collective-permute-start | bytes 1677320 | tf_op jit(solution)/shard_map/ppermute | solution.py:31
  78.6 33.9 %collective-permute-start.12 = (f32[4,34944]{1,0:T(4,128)S(1)}, f32[4,34944]{1,0:T(4,128)S(1)}, u32[]{:S(2)}, u32[]{:S(2)}) collective-permute-start(f32[4,34944]{1,0:T(4,128)S(1)} %collective-permute-done.8.refs_0_), channel_id=1, source_target_pairs={{0,4},{4,0},{8,12},{12,8},{16,20},{20,16},{24,28},{28,24},{1,5},{5... | collective-permute-start | bytes 1677320 | tf_op jit(solution)/shard_map/ppermute | solution.py:31
  98.0 12.3 %collective-permute-start.3 = (f32[4,34944]{1,0:T(4,128)S(1)}, f32[4,34944]{1,0:T(4,128)S(1)}, u32[]{:S(2)}, u32[]{:S(2)}) collective-permute-start(f32[4,34944]{1,0:T(4,128)S(1)} %collective-permute-done.2.refs_2_), channel_id=1, source_target_pairs={{0,2},{1,3},{2,0},{3,1},{4,6},{5,7},{6,4},{7,5},{8,10},{9,11},{10,... | collective-permute-start | bytes 1677320 | tf_op jit(solution)/shard_map/ppermute | solution.py:31
  99.2 13.5 %collective-permute-start.9 = (f32[4,34944]{1,0:T(4,128)S(1)}, f32[4,34944]{1,0:T(4,128)S(1)}, u32[]{:S(2)}, u32[]{:S(2)}) collective-permute-start(f32[4,34944]{1,0:T(4,128)S(1)} %collective-permute-done.1.refs_1_), channel_id=1, source_target_pairs={{0,8},{4,12},{8,0},{12,4},{16,24},{20,28},{24,16},{28,20},{1,9},{5... | collective-permute-start | bytes 1677320 | tf_op jit(solution)/shard_map/ppermute | solution.py:31
  99.3 14.8 %collective-permute-start.6 = (f32[4,34944]{1,0:T(4,128)S(1)}, f32[4,34944]{1,0:T(4,128)S(1)}, u32[]{:S(2)}, u32[]{:S(2)}) collective-permute-start(f32[4,34944]{1,0:T(4,128)S(1)} %collective-permute-done.2.refs_2_), channel_id=1, source_target_pairs={{0,4},{4,0},{8,12},{12,8},{16,20},{20,16},{24,28},{28,24},{1,5},{5... | collective-permute-start | bytes 1677320 | tf_op jit(solution)/shard_map/ppermute | solution.py:31
  101.7 106.9 %collective-permute-start.14 = (f32[4,34944]{1,0:T(4,128)S(1)}, f32[4,34944]{1,0:T(4,128)S(1)}, u32[]{:S(2)}, u32[]{:S(2)}) collective-permute-start(f32[4,34944]{1,0:T(4,128)S(1)} %collective-permute-done.10.refs_2_), channel_id=1, source_target_pairs={{0,4},{4,0},{8,12},{12,8},{16,20},{20,16},{24,28},{28,24},{1,5},{5... | collective-permute-start | bytes 1677320 | tf_op jit(solution)/shard_map/ppermute | solution.py:31
  110.3 98.4 %collective-permute-start.5 = (f32[4,34944]{1,0:T(4,128)S(1)}, f32[4,34944]{1,0:T(4,128)S(1)}, u32[]{:S(2)}, u32[]{:S(2)}) collective-permute-start(f32[4,34944]{1,0:T(4,128)S(1)} %collective-permute-done.1.refs_1_), channel_id=1, source_target_pairs={{0,4},{4,0},{8,12},{12,8},{16,20},{20,16},{24,28},{28,24},{1,5},{5... | collective-permute-start | bytes 1677320 | tf_op jit(solution)/shard_map/ppermute | solution.py:31
  112.6 96.0 %collective-permute-start.15 = (f32[4,34944]{1,0:T(4,128)S(1)}, f32[4,34944]{1,0:T(4,128)S(1)}, u32[]{:S(2)}, u32[]{:S(2)}) collective-permute-start(f32[4,34944]{1,0:T(4,128)S(1)} %collective-permute-done.11.refs_3_), channel_id=1, source_target_pairs={{0,4},{4,0},{8,12},{12,8},{16,20},{20,16},{24,28},{28,24},{1,5},{5... | collective-permute-start | bytes 1677320 | tf_op jit(solution)/shard_map/ppermute | solution.py:31
  112.7 96.0 %collective-permute-start.13 = (f32[4,34944]{1,0:T(4,128)S(1)}, f32[4,34944]{1,0:T(4,128)S(1)}, u32[]{:S(2)}, u32[]{:S(2)}) collective-permute-start(f32[4,34944]{1,0:T(4,128)S(1)} %collective-permute-done.12.refs_0_), channel_id=1, source_target_pairs={{0,2},{1,3},{2,0},{3,1},{4,6},{5,7},{6,4},{7,5},{8,10},{9,11},{10,... | collective-permute-start | bytes 1677320 | tf_op jit(solution)/shard_map/ppermute | solution.py:31
  114.2 94.5 %collective-permute-start.7 = (f32[4,34944]{1,0:T(4,128)S(1)}, f32[4,34944]{1,0:T(4,128)S(1)}, u32[]{:S(2)}, u32[]{:S(2)}) collective-permute-start(f32[4,34944]{1,0:T(4,128)S(1)} %collective-permute-done.6.refs_2_), channel_id=1, source_target_pairs={{0,2},{1,3},{2,0},{3,1},{4,6},{5,7},{6,4},{7,5},{8,10},{9,11},{10,... | collective-permute-start | bytes 1677320 | tf_op jit(solution)/shard_map/ppermute | solution.py:31
  205.9 2.7 copy-start
  254.5 2.7 copy-start.1
  302.9 2.6 copy-start.2
  329.7 10.7 %collective-permute-start.16 = (f32[2,1,512,1024]{3,2,1,0:T(8,128)}, f32[2,1,512,1024]{3,2,1,0:T(8,128)}, u32[]{:S(2)}, u32[]{:S(2)}) collective-permute-start(f32[2,1,512,1024]{3,2,1,0:T(8,128)} %columns_transform.3.refs_0_), channel_id=1, source_target_pairs={{0,1},{1,0},{2,3},{3,2},{4,5},{5,4},{6,7},{7,6},{8,9},{9,8},{10,11... | collective-permute-start | bytes 12582920 | tf_op jit(solution)/shard_map/ppermute | solution.py:31
  333.0 13.1 %collective-permute-start.17 = (f32[2,1,512,1024]{3,2,1,0:T(8,128)}, f32[2,1,512,1024]{3,2,1,0:T(8,128)}, u32[]{:S(2)}, u32[]{:S(2)}) collective-permute-start(f32[2,1,512,1024]{3,2,1,0:T(8,128)} %columns_transform.4.refs_1_), channel_id=1, source_target_pairs={{0,1},{1,0},{2,3},{3,2},{4,5},{5,4},{6,7},{7,6},{8,9},{9,8},{10,11... | collective-permute-start | bytes 12582920 | tf_op jit(solution)/shard_map/ppermute | solution.py:31
  333.0 19.0 %collective-permute-start.18 = (f32[2,1,512,1024]{3,2,1,0:T(8,128)}, f32[2,1,512,1024]{3,2,1,0:T(8,128)}, u32[]{:S(2)}, u32[]{:S(2)}) collective-permute-start(f32[2,1,512,1024]{3,2,1,0:T(8,128)} %columns_transform.5.refs_2_), channel_id=1, source_target_pairs={{0,1},{1,0},{2,3},{3,2},{4,5},{5,4},{6,7},{7,6},{8,9},{9,8},{10,11... | collective-permute-start | bytes 12582920 | tf_op jit(solution)/shard_map/ppermute | solution.py:31
